TPU v7x, 128 devices: a whole 4x4x4 slice. The times are simulated.
128 devices in a mesh: beam: 16 (over x, z_hi, core), freq: 8 (over z_lo, y).
Axes of the slice: x: 4, y: 4, z: 4 (z_hi: 2, z_lo: 2; z = z_hi * 2 + z_lo), core: 2. Of those that a mesh axis runs over, the one named last changes fastest.
Arguments:
- intensity: bfloat16 [16, 16384, 256], P(None, ('freq', 'beam')), may hold values from -600 to 600, as said below
- channel_mask: int32 [16384], P('freq'), may hold values 0 or 1
- box_widths: int32 [9], replicated, may hold values from 1 to 64
Outputs:
- snr_peak: float32 [16, 4096], P('beam', 'freq')
Inputs may be any that keep to these rules, and one draw needn't show every extreme that they name: `intensity`: filterbank intensities of every beam and channel, of any sign.
All inputs are finite; a program needn't handle non-finite values. No bound on the sum of `channel_mask` on one device may be relied on, other than what follows from the above.
Results may differ from a plain program's by a relative error of at most 0.002.
Values may be sent and summed in bfloat16 or wider, within the bound.
No kernel may reach another device: no remote copies, remote signals or barrier semaphores. Data moves between devices by JAX's collectives and lax.ppermute only.
A program may use at most 64 MiB of HBM per device.

v0:
```python
import functools

import jax
import jax.numpy as jnp
from jax import lax
from jax.experimental import pallas as pl
from jax.experimental.pallas import tpu as pltpu
from jax.sharding import PartitionSpec as P

CHANS = 16384
EPSILON = 1e-05
LANES = 128
CHUNKS = 4


def shifted(first, second, amount, inside):
    first = pltpu.roll(first, amount, 1)
    second = pltpu.roll(second, amount, 1)
    return jnp.where(inside, first, second), jnp.where(inside, second, 0.0)


def channel_kernel(x_hbm, mask_ref, out_ref, xbuf, sems, sums, squares, level2, rows32):
    beams, chans, samples = xbuf.shape
    step = chans // CHUNKS
    copies = []
    for k in range(CHUNKS):
        part = pl.ds(k * step, step)
        copies.append(pltpu.make_async_copy(x_hbm.at[:, part, :], xbuf.at[:, part, :], sems.at[k]))
        copies[-1].start()
    for k in range(CHUNKS):
        copies[k].wait()
        for c in range(k * step, (k + 1) * step, 16):
            total = square = None
            for b in range(beams):
                v = xbuf[b, c : c + 16, :].astype(jnp.float32)
                total = v if total is None else total + v
                square = v * v if square is None else square + v * v
            sums[c : c + 16, :] = total[:, :LANES] + total[:, LANES:]
            squares[c : c + 16, :] = square[:, :LANES] + square[:, LANES:]
    count = float(beams * samples)
    mean = jnp.sum(sums[...].T, axis=0, keepdims=True) / count
    var = jnp.sum(squares[...].T, axis=0, keepdims=True) / count - mean * mean
    mask = mask_ref[pl.ds(lax.axis_index("beam"), 1), :].astype(jnp.float32)
    scale = lax.rsqrt(var + EPSILON) * mask
    bands = chans // 4
    row = lax.broadcasted_iota(jnp.int32, (bands, chans), 0)
    chan = lax.broadcasted_iota(jnp.int32, (bands, chans), 1)
    weight = jnp.where(chan // 4 == row, scale, 0.0)
    high = weight.astype(jnp.bfloat16)
    rest = (weight - high.astype(jnp.float32)).astype(jnp.bfloat16)
    held = high.astype(jnp.float32) + rest.astype(jnp.float32)
    offset = jnp.sum(held * mean, axis=1, keepdims=True)
    both = jnp.concatenate([high, rest], axis=0)
    for b in range(beams):
        y = jnp.dot(both, xbuf[b], preferred_element_type=jnp.float32)
        y = y[:bands] + y[bands:] - offset
        level2[0, b * bands : (b + 1) * bands, :] = y[:, :LANES]
        level2[1, b * bands : (b + 1) * bands, :] = y[:, LANES:]
    lane = lax.broadcasted_iota(jnp.int32, (8, LANES), 1)

    def subband(tile, level, s):
        if level == 2:
            at = pl.ds(tile * 8 * bands + s, 8, stride=bands)
            return [(level2[0, at, :], level2[1, at, :])]
        low = subband(tile, level - 1, 2 * s)
        high = subband(tile, level - 1, 2 * s + 1)
        rows = []
        for r in range(len(low)):
            for shift in (r, r + 1):
                moved = high[r]
                if shift:
                    moved = shifted(*high[r], LANES - shift, lane < LANES - shift)
                rows.append((low[r][0] + moved[0], low[r][1] + moved[1]))
        return rows

    for tile in range(beams // 8):
        rows = subband(tile, 7, 0)
        for r, halves in enumerate(rows):
            for h in range(2):
                start = ((r // 4) * beams + tile * 8) * 8 + (r % 4) * 2 + h
                rows32[pl.ds(start, 8, stride=8), :] = halves[h]
    out_ref[...] = rows32[...].astype(jnp.bfloat16)


def trial_kernel(rows_ref, widths_ref, out_ref, rows32, level11, trials, prefix):
    f = lax.axis_index("freq")
    rows32[...] = rows_ref[...].astype(jnp.float32)
    lane = lax.broadcasted_iota(jnp.int32, (8, LANES), 1)
    sub = lax.broadcasted_iota(jnp.int32, (8, LANES), 0)
    zero = jnp.zeros((8, LANES), jnp.float32)

    bands = []
    for u in range(16):
        bands.append([
            tuple(rows32[pl.ds(u * 8 + i * 2 + h, 8, stride=128), :] for h in range(2)) for i in range(4)
        ])
    parents = 4
    while len(bands) > 1:
        base = f * parents
        late = None
        if len(bands) == 2:
            late = base >= LANES
            base = jnp.where(late, base - LANES, base)
        moves = []
        for i in range(parents + 1):
            s = base + i
            moves.append(((LANES - s) & (LANES - 1), lane < LANES - s))
        merged = []
        for low, high in zip(bands[0::2], bands[1::2]):
            out = []
            for i in range(parents):
                first, second = high[i]
                if late is not None:
                    first = jnp.where(late, second, first)
                    second = jnp.where(late, zero, second)
                for amount, inside in (moves[i], moves[i + 1]):
                    a, b = shifted(first, second, amount, inside)
                    out.append((low[i][0] + a, low[i][1] + b))
            merged.append(out)
        bands = merged
        parents *= 2
    for j in range(parents):
        first, second = bands[0][j]
        for bit in range(3):
            s = (f * parents + j) << bit
            q = s // LANES
            a = jnp.where(q == 0, first, jnp.where(q == 1, second, zero))
            b = jnp.where(q == 0, second, zero)
            s = s & (LANES - 1)
            a, b = shifted(a, b, (LANES - s) & (LANES - 1), lane < LANES - s)
            chosen = (sub >> bit & 1) == 1
            first = jnp.where(chosen, a, first)
            second = jnp.where(chosen, b, second)
        level11[0, j * 8 : j * 8 + 8, :] = first
        level11[1, j * 8 : j * 8 + 8, :] = second

    def ahead(pair, s):
        return shifted(*pair, LANES - s, lane < LANES - s) if s else pair

    def added(low, high):
        return low[0] + high[0], low[1] + high[1]

    for jt in range(8):
        tiles = []
        for band in range(8):
            at = pl.ds(jt * 64 + band, 8, stride=8)
            tiles.append((level11[0, at, :], level11[1, at, :]))
        l12 = [[added(tiles[2 * k], ahead(tiles[2 * k + 1], e)) for e in range(2)] for k in range(4)]
        l13 = [
            [added(l12[2 * k][e >> 1], ahead(l12[2 * k + 1][e >> 1], (e + 1) // 2)) for e in range(4)]
            for k in range(2)
        ]
        for c in range(8):
            pair = added(l13[0][c >> 1], ahead(l13[1][c >> 1], (c + 1) // 2))
            at = pl.ds(jt * 64 + c, 8, stride=8)
            for h in range(2):
                trials[h, at, :] = pair[h]

    count = trials.shape[1]
    samples = 2 * LANES
    top = prefix.shape[1]
    parts = []
    for h in range(2):
        d = trials[h]
        high = d.astype(jnp.bfloat16)
        parts.append((high, (d - high.astype(jnp.float32)).astype(jnp.bfloat16)))
    values = jnp.concatenate([parts[0][0], parts[1][0], parts[0][1], parts[1][1]], axis=1)
    size = (samples + 16, 4 * LANES)
    step = lax.broadcasted_iota(jnp.int32, size, 0)
    time = lax.broadcasted_iota(jnp.int32, size, 1) & (samples - 1)
    lower = jnp.where(time < step, 1.0, 0.0).astype(jnp.bfloat16)
    summed = lax.dot_general(lower, values, (((1,), (1,)), ((), ())), preferred_element_type=jnp.float32)
    for lt in range(count // LANES):
        prefix[lt, : samples + 8, :] = summed[: samples + 8, lt * LANES : (lt + 1) * LANES]
        prefix[lt, samples : samples + 8, :] = jnp.where(
            sub == 0, summed[samples : samples + 8, lt * LANES : (lt + 1) * LANES], -jnp.inf
        )
        prefix[lt, samples + 8 :, :] = jnp.full((top - samples - 8, LANES), -jnp.inf, jnp.float32)
    for lt in range(count // LANES):
        starts = [prefix[lt, t : t + 8, :] for t in range(0, samples, 8)]
        best = None
        for k in range(widths_ref.shape[0]):
            w = widths_ref[k]
            peak = None
            for n, start in enumerate(starts):
                box = prefix[lt, pl.ds(8 * n + w, 8), :] - start
                peak = box if peak is None else jnp.maximum(peak, box)
            peak = peak * lax.rsqrt(jnp.full((8, LANES), w * CHANS, jnp.int32).astype(jnp.float32))
            best = peak if best is None else jnp.maximum(best, peak)
        out_ref[:, lt * LANES : (lt + 1) * LANES] = jnp.max(best, axis=0, keepdims=True)


def shards(intensity, channel_mask, box_widths):
    beams, chans, samples = intensity.shape
    devices = lax.axis_size("beam") * lax.axis_size("freq")
    rows = pl.pallas_call(
        channel_kernel,
        out_shape=jax.ShapeDtypeStruct((devices * 8, LANES), jnp.bfloat16),
        in_specs=[pl.BlockSpec(memory_space=pl.ANY), pl.BlockSpec(memory_space=pltpu.VMEM)],
        out_specs=pl.BlockSpec(memory_space=pltpu.VMEM),
        scratch_shapes=[
            pltpu.VMEM((beams, chans, samples), jnp.bfloat16),
            pltpu.SemaphoreType.DMA((CHUNKS,)),
            pltpu.VMEM((chans, LANES), jnp.float32),
            pltpu.VMEM((chans, LANES), jnp.float32),
            pltpu.VMEM((2, beams * chans // 4, LANES), jnp.float32),
            pltpu.VMEM((devices * 8, LANES), jnp.float32),
        ],
        compiler_params=pltpu.CompilerParams(vmem_limit_bytes=32 * 1024 * 1024),
        name="channel_levels",
    )(intensity, channel_mask.reshape(-1, LANES))
    rows = lax.all_to_all(rows.reshape(devices, 8, LANES), ("freq", "beam"), 0, 0, tiled=True)
    return pl.pallas_call(
        trial_kernel,
        out_shape=jax.ShapeDtypeStruct((1, 4 * LANES), jnp.float32),
        in_specs=[pl.BlockSpec(memory_space=pltpu.VMEM), pl.BlockSpec(memory_space=pltpu.SMEM)],
        out_specs=pl.BlockSpec(memory_space=pltpu.VMEM),
        scratch_shapes=[
            pltpu.VMEM((devices * 8, LANES), jnp.float32),
            pltpu.VMEM((2, 512, LANES), jnp.float32),
            pltpu.VMEM((2, 512, LANES), jnp.float32),
            pltpu.VMEM((4, 2 * LANES + 72, LANES), jnp.float32),
        ],
        compiler_params=pltpu.CompilerParams(vmem_limit_bytes=32 * 1024 * 1024),
        name="trial_levels",
    )(rows.reshape(devices * 8, LANES), box_widths)


def solution(mesh):
    in_specs = (P(None, ("freq", "beam"), None), P("freq"), P())
    out_specs = P("beam", "freq")
    return jax.shard_map(shards, mesh=mesh, in_specs=in_specs, out_specs=out_specs, check_vma=False)
```

profile of v0, /device:TPU:1, one launch (start us, length us, event | category | flops | bytes accessed | tf_op | source)
XLA Modules:
  0.0 32.0 jit_solution(1178334707140979414)
XLA Ops:
  0.0 0.0 copy-start
  0.0 1.2 %copy-done = bf16[16,128,256]{2,1,0:T(8,128)(2,1)S(1)} copy-done((bf16[16,128,256]{2,1,0:T(8,128)(2,1)S(1)}, bf16[16,128,256]{2,1,0:T(8,128)(2,1)}, u32[]{:S(2)}) %copy-start) | copy-done | bytes 1048600
  1.2 0.0 copy-start.1
  1.2 0.7 %copy-done.1 = s32[2048]{0:T(1024)S(1)} copy-done((s32[2048]{0:T(1024)S(1)}, s32[2048]{0:T(1024)}, u32[]{:S(2)}) %copy-start.1) | copy-done | bytes 8216
  1.9 1.4 %channel_levels.1 = bf16[1024,128]{1,0:T(8,128)(2,1)S(1)} custom-call(bf16[16,128,256]{2,1,0:T(8,128)(2,1)S(1)} %copy-done, s32[16,128]{1,0:T(8,128)S(1)} %bitcast.5), custom_call_target="tpu_custom_call" | custom-call | tf_op jit(solution)/shard_map/channel_levels/pallas_call | solution.py:196
  3.3 22.1 %all_to_all.5 = bf16[128,8,128]{2,1,0:T(8,128)(2,1)S(1)} all-to-all(bf16[128,8,128]{2,1,0:T(8,128)(2,1)S(1)} %bitcast.3), channel_id=1, replica_groups=mesh['beam'=16,'freq'=8] {'freq','beam'}, dimensions={0} | all-to-all | bytes 524288 | tf_op jit(solution)/shard_map/all_to_all | solution.py:212
  25.4 0.0 copy-start.2
  25.5 0.7 %copy-done.2 = s32[9]{0:T(128)S(1)} copy-done((s32[9]{0:T(128)S(1)}, s32[9]{0:T(128)}, u32[]{:S(2)}) %copy-start.2) | copy-done | bytes 60
  26.1 5.9 %trial_levels.1 = f32[1,512]{1,0:T(1,128)} custom-call(bf16[1024,128]{1,0:T(8,128)(2,1)S(1)} %bitcast.4, s32[9]{0:T(128)S(1)} %copy-done.2), custom_call_target="tpu_custom_call" | custom-call | tf_op jit(solution)/shard_map/trial_levels/pallas_call | solution.py:213
Async XLA Ops:
  0.0 1.2 %copy-start = (bf16[16,128,256]{2,1,0:T(8,128)(2,1)S(1)}, bf16[16,128,256]{2,1,0:T(8,128)(2,1)}, u32[]{:S(2)}) copy-start(bf16[16,128,256]{2,1,0:T(8,128)(2,1)} %x_hbm.1) | copy-start | bytes 3145732
  1.2 0.7 %copy-start.1 = (s32[2048]{0:T(1024)S(1)}, s32[2048]{0:T(1024)}, u32[]{:S(2)}) copy-start(s32[2048]{0:T(1024)} %param.4) | copy-start | bytes 24580
  25.4 0.7 %copy-start.2 = (s32[9]{0:T(128)S(1)}, s32[9]{0:T(128)}, u32[]{:S(2)}) copy-start(s32[9]{0:T(128)} %widths_ref.1) | copy-start | bytes 112
where the time goes:
time: 32.3 us; the launch traced here: 32 us
  blocking collectives  22.1 us (68%)
  Pallas kernels  7.32 us (23%)
  local copies, waits for them, and re-layouts  2.58 us (8%)
    all_to_all x1, blocking collectives, shards(): lax.all_to_all(rows.reshape(devices, 8, LANES), ('freq', 'beam'), 0, 0, t...  22.1 us
    pallas_call x1, Pallas kernels, shards(): pl.pallas_call(trial_kernel, out_shape=jax.ShapeDtypeStruct((1, 4 * LANES...  5.93 us
    unnamed x6, local copies, waits for them, and re-layouts  2.58 us
    pallas_call x1, Pallas kernels, shards(): pl.pallas_call(channel_kernel, out_shape=jax.ShapeDtypeStruct((devices *...  1.39 us

commit v1 on v0

--- a/solution.py
+++ b/solution.py
@@ -11,6 +11,8 @@
 EPSILON = 1e-05
 LANES = 128
 CHUNKS = 4
+SKEW = 16
+TAIL = 4
 
 
 def shifted(first, second, amount, inside):
@@ -19,7 +21,7 @@
     return jnp.where(inside, first, second), jnp.where(inside, second, 0.0)
 
 
-def channel_kernel(x_hbm, mask_ref, out_ref, xbuf, sems, sums, squares, level2, rows32):
+def channel_kernel(x_hbm, mask_hbm, out_ref, xbuf, masks, sems, sums, squares, level2, rows32):
     beams, chans, samples = xbuf.shape
     step = chans // CHUNKS
     copies = []
@@ -27,6 +29,8 @@
         part = pl.ds(k * step, step)
         copies.append(pltpu.make_async_copy(x_hbm.at[:, part, :], xbuf.at[:, part, :], sems.at[k]))
         copies[-1].start()
+    copies.append(pltpu.make_async_copy(mask_hbm, masks, sems.at[CHUNKS]))
+    copies[-1].start()
     for k in range(CHUNKS):
         copies[k].wait()
         for c in range(k * step, (k + 1) * step, 16):
@@ -40,7 +44,8 @@
     count = float(beams * samples)
     mean = jnp.sum(sums[...].T, axis=0, keepdims=True) / count
     var = jnp.sum(squares[...].T, axis=0, keepdims=True) / count - mean * mean
-    mask = mask_ref[pl.ds(lax.axis_index("beam"), 1), :].astype(jnp.float32)
+    copies[CHUNKS].wait()
+    mask = masks[pl.ds(lax.axis_index("beam"), 1), :].astype(jnp.float32)
     scale = lax.rsqrt(var + EPSILON) * mask
     bands = chans // 4
     row = lax.broadcasted_iota(jnp.int32, (bands, chans), 0)
@@ -82,7 +87,9 @@
     out_ref[...] = rows32[...].astype(jnp.bfloat16)
 
 
-def trial_kernel(rows_ref, widths_ref, out_ref, rows32, level11, trials, prefix):
+def trial_kernel(rows_ref, widths_hbm, out_ref, widths, sem, rows32, level11, skewed, trials, prefix):
+    copy = pltpu.make_async_copy(widths_hbm, widths, sem)
+    copy.start()
     f = lax.axis_index("freq")
     rows32[...] = rows_ref[...].astype(jnp.float32)
     lane = lax.broadcasted_iota(jnp.int32, (8, LANES), 1)
@@ -120,19 +127,26 @@
         bands = merged
         parents *= 2
     for j in range(parents):
-        first, second = bands[0][j]
-        for bit in range(3):
-            s = (f * parents + j) << bit
-            q = s // LANES
-            a = jnp.where(q == 0, first, jnp.where(q == 1, second, zero))
-            b = jnp.where(q == 0, second, zero)
-            s = s & (LANES - 1)
-            a, b = shifted(a, b, (LANES - s) & (LANES - 1), lane < LANES - s)
-            chosen = (sub >> bit & 1) == 1
-            first = jnp.where(chosen, a, first)
-            second = jnp.where(chosen, b, second)
-        level11[0, j * 8 : j * 8 + 8, :] = first
-        level11[1, j * 8 : j * 8 + 8, :] = second
+        for h in range(2):
+            level11[h, j * 8 : j * 8 + 8, :] = bands[0][j][h]
+
+    def skew(block, carry):
+        for n in range(SKEW):
+            j = block * SKEW + n
+            at = pl.ds(pl.multiple_of(j * 8, 8), 8)
+            first, second = level11[0, at, :], level11[1, at, :]
+            time = lane + sub * (f * parents + j)
+            moved = time & (LANES - 1)
+            first = jnp.take_along_axis(first, moved, axis=1, mode="promise_in_bounds")
+            second = jnp.take_along_axis(second, moved, axis=1, mode="promise_in_bounds")
+            inside = time < LANES
+            first = jnp.where(inside, first, jnp.where(time < 2 * LANES, second, 0.0))
+            second = jnp.where(inside, second, 0.0)
+            skewed[0, at, :] = first
+            skewed[1, at, :] = second
+        return carry
+
+    lax.fori_loop(0, parents // SKEW, skew, 0)
 
     def ahead(pair, s):
         return shifted(*pair, LANES - s, lane < LANES - s) if s else pair
@@ -140,11 +154,16 @@
     def added(low, high):
         return low[0] + high[0], low[1] + high[1]
 
-    for jt in range(8):
+    def last_levels(block, carry):
+        for n in range(TAIL):
+            last_tile(block * TAIL + n)
+        return carry
+
+    def last_tile(jt):
         tiles = []
         for band in range(8):
             at = pl.ds(jt * 64 + band, 8, stride=8)
-            tiles.append((level11[0, at, :], level11[1, at, :]))
+            tiles.append((skewed[0, at, :], skewed[1, at, :]))
         l12 = [[added(tiles[2 * k], ahead(tiles[2 * k + 1], e)) for e in range(2)] for k in range(4)]
         l13 = [
             [added(l12[2 * k][e >> 1], ahead(l12[2 * k + 1][e >> 1], (e + 1) // 2)) for e in range(4)]
@@ -155,6 +174,8 @@
             at = pl.ds(jt * 64 + c, 8, stride=8)
             for h in range(2):
                 trials[h, at, :] = pair[h]
+
+    lax.fori_loop(0, 8 // TAIL, last_levels, 0)
 
     count = trials.shape[1]
     samples = 2 * LANES
@@ -176,11 +197,12 @@
             sub == 0, summed[samples : samples + 8, lt * LANES : (lt + 1) * LANES], -jnp.inf
         )
         prefix[lt, samples + 8 :, :] = jnp.full((top - samples - 8, LANES), -jnp.inf, jnp.float32)
+    copy.wait()
     for lt in range(count // LANES):
         starts = [prefix[lt, t : t + 8, :] for t in range(0, samples, 8)]
         best = None
-        for k in range(widths_ref.shape[0]):
-            w = widths_ref[k]
+        for k in range(widths.shape[0]):
+            w = widths[k]
             peak = None
             for n, start in enumerate(starts):
                 box = prefix[lt, pl.ds(8 * n + w, 8), :] - start
@@ -190,17 +212,22 @@
         out_ref[:, lt * LANES : (lt + 1) * LANES] = jnp.max(best, axis=0, keepdims=True)
 
 
+def in_hbm(array):
+    return pltpu.with_memory_space_constraint(array, pltpu.HBM)
+
+
 def shards(intensity, channel_mask, box_widths):
     beams, chans, samples = intensity.shape
     devices = lax.axis_size("beam") * lax.axis_size("freq")
     rows = pl.pallas_call(
         channel_kernel,
         out_shape=jax.ShapeDtypeStruct((devices * 8, LANES), jnp.bfloat16),
-        in_specs=[pl.BlockSpec(memory_space=pl.ANY), pl.BlockSpec(memory_space=pltpu.VMEM)],
+        in_specs=[pl.BlockSpec(memory_space=pltpu.HBM), pl.BlockSpec(memory_space=pltpu.HBM)],
         out_specs=pl.BlockSpec(memory_space=pltpu.VMEM),
         scratch_shapes=[
             pltpu.VMEM((beams, chans, samples), jnp.bfloat16),
-            pltpu.SemaphoreType.DMA((CHUNKS,)),
+            pltpu.VMEM((chans * lax.axis_size("beam") // LANES, LANES), jnp.int32),
+            pltpu.SemaphoreType.DMA((CHUNKS + 1,)),
             pltpu.VMEM((chans, LANES), jnp.float32),
             pltpu.VMEM((chans, LANES), jnp.float32),
             pltpu.VMEM((2, beams * chans // 4, LANES), jnp.float32),
@@ -208,22 +235,25 @@
         ],
         compiler_params=pltpu.CompilerParams(vmem_limit_bytes=32 * 1024 * 1024),
         name="channel_levels",
-    )(intensity, channel_mask.reshape(-1, LANES))
+    )(in_hbm(intensity), in_hbm(channel_mask.reshape(-1, LANES)))
     rows = lax.all_to_all(rows.reshape(devices, 8, LANES), ("freq", "beam"), 0, 0, tiled=True)
     return pl.pallas_call(
         trial_kernel,
         out_shape=jax.ShapeDtypeStruct((1, 4 * LANES), jnp.float32),
-        in_specs=[pl.BlockSpec(memory_space=pltpu.VMEM), pl.BlockSpec(memory_space=pltpu.SMEM)],
+        in_specs=[pl.BlockSpec(memory_space=pltpu.VMEM), pl.BlockSpec(memory_space=pltpu.HBM)],
         out_specs=pl.BlockSpec(memory_space=pltpu.VMEM),
         scratch_shapes=[
+            pltpu.SMEM(box_widths.shape, jnp.int32),
+            pltpu.SemaphoreType.DMA,
             pltpu.VMEM((devices * 8, LANES), jnp.float32),
+            pltpu.VMEM((2, 512, LANES), jnp.float32),
             pltpu.VMEM((2, 512, LANES), jnp.float32),
             pltpu.VMEM((2, 512, LANES), jnp.float32),
             pltpu.VMEM((4, 2 * LANES + 72, LANES), jnp.float32),
         ],
         compiler_params=pltpu.CompilerParams(vmem_limit_bytes=32 * 1024 * 1024),
         name="trial_levels",
-    )(rows.reshape(devices * 8, LANES), box_widths)
+    )(rows.reshape(devices * 8, LANES), in_hbm(box_widths))
 
 
 def solution(mesh):

time: 32.3 us -> 28 us (0.87)
  local copies, waits for them, and re-layouts: 2.58 us -> 0 us
  Pallas kernels: 7.32 us -> 5.68 us
    pallas_call x1, Pallas kernels: 5.93 us -> 3.31 us  [shards(): pl.pallas_call(trial_kernel, out_shape=jax.ShapeDtypeStruct((1, 4 * LANES...]
    unnamed x6 -> x0, local copies, waits for them, and re-layouts: 2.58 us -> none
    pallas_call x1, Pallas kernels: 1.39 us -> 2.37 us  [shards(): pl.pallas_call(channel_kernel, out_shape=jax.ShapeDtypeStruct((devices *...]
where the time goes in v1:
time: 28 us; the launch traced here: 27.8 us
  blocking collectives  22.1 us (79%)
  Pallas kernels  5.68 us (20%)
    all_to_all x1, blocking collectives, shards(): lax.all_to_all(rows.reshape(devices, 8, LANES), ('freq', 'beam'), 0, 0, t...  22.1 us
    pallas_call x1, Pallas kernels, shards(): pl.pallas_call(trial_kernel, out_shape=jax.ShapeDtypeStruct((1, 4 * LANES...  3.31 us
    pallas_call x1, Pallas kernels, shards(): pl.pallas_call(channel_kernel, out_shape=jax.ShapeDtypeStruct((devices *...  2.37 us

profile of v1, /device:TPU:1, one launch (start us, length us, event | category | flops | bytes accessed | tf_op | source)
XLA Modules:
  0.0 27.8 jit_solution(9934413524220681016)
XLA Ops:
  0.0 2.4 %channel_levels.1 = bf16[1024,128]{1,0:T(8,128)(2,1)S(1)} custom-call(bf16[16,128,256]{2,1,0:T(8,128)(2,1)} %x_hbm.1, s32[16,128]{1,0:T(8,128)} %bitcast.5), custom_call_target="tpu_custom_call" | custom-call | tf_op jit(solution)/shard_map/channel_levels/pallas_call | solution.py:222
  2.4 22.1 %all_to_all.5 = bf16[128,8,128]{2,1,0:T(8,128)(2,1)S(1)} all-to-all(bf16[128,8,128]{2,1,0:T(8,128)(2,1)S(1)} %bitcast.3), channel_id=1, replica_groups=mesh['beam'=16,'freq'=8] {'freq','beam'}, dimensions={0} | all-to-all | bytes 524288 | tf_op jit(solution)/shard_map/all_to_all | solution.py:239
  24.5 3.3 %trial_levels.1 = f32[1,512]{1,0:T(1,128)} custom-call(bf16[1024,128]{1,0:T(8,128)(2,1)S(1)} %bitcast.4, s32[9]{0:T(128)} %widths_hbm.1), custom_call_target="tpu_custom_call" | custom-call | tf_op jit(solution)/shard_map/trial_levels/pallas_call | solution.py:240

commit v2 on v1

--- a/solution.py
+++ b/solution.py
@@ -11,8 +11,7 @@
 EPSILON = 1e-05
 LANES = 128
 CHUNKS = 4
-SKEW = 16
-TAIL = 4
+WIDTHS = 9
 
 
 def shifted(first, second, amount, inside):
@@ -82,104 +81,68 @@
         rows = subband(tile, 7, 0)
         for r, halves in enumerate(rows):
             for h in range(2):
-                start = ((r // 4) * beams + tile * 8) * 8 + (r % 4) * 2 + h
+                start = ((r // 4) * beams + tile * 8) * 8 + h * 4 + r % 4
                 rows32[pl.ds(start, 8, stride=8), :] = halves[h]
     out_ref[...] = rows32[...].astype(jnp.bfloat16)
 
 
-def trial_kernel(rows_ref, widths_hbm, out_ref, widths, sem, rows32, level11, skewed, trials, prefix):
+def trial_kernel(rows_ref, widths_hbm, out_ref, widths, sem, rows32, level11, trials, prefix):
     copy = pltpu.make_async_copy(widths_hbm, widths, sem)
     copy.start()
     f = lax.axis_index("freq")
     rows32[...] = rows_ref[...].astype(jnp.float32)
     lane = lax.broadcasted_iota(jnp.int32, (8, LANES), 1)
     sub = lax.broadcasted_iota(jnp.int32, (8, LANES), 0)
-    zero = jnp.zeros((8, LANES), jnp.float32)
-
-    bands = []
-    for u in range(16):
-        bands.append([
-            tuple(rows32[pl.ds(u * 8 + i * 2 + h, 8, stride=128), :] for h in range(2)) for i in range(4)
-        ])
-    parents = 4
-    while len(bands) > 1:
-        base = f * parents
-        late = None
-        if len(bands) == 2:
-            late = base >= LANES
-            base = jnp.where(late, base - LANES, base)
-        moves = []
-        for i in range(parents + 1):
-            s = base + i
-            moves.append(((LANES - s) & (LANES - 1), lane < LANES - s))
-        merged = []
-        for low, high in zip(bands[0::2], bands[1::2]):
-            out = []
-            for i in range(parents):
-                first, second = high[i]
-                if late is not None:
-                    first = jnp.where(late, second, first)
-                    second = jnp.where(late, zero, second)
-                for amount, inside in (moves[i], moves[i + 1]):
-                    a, b = shifted(first, second, amount, inside)
-                    out.append((low[i][0] + a, low[i][1] + b))
-            merged.append(out)
-        bands = merged
-        parents *= 2
-    for j in range(parents):
-        for h in range(2):
-            level11[h, j * 8 : j * 8 + 8, :] = bands[0][j][h]
-
-    def skew(block, carry):
-        for n in range(SKEW):
-            j = block * SKEW + n
-            at = pl.ds(pl.multiple_of(j * 8, 8), 8)
-            first, second = level11[0, at, :], level11[1, at, :]
-            time = lane + sub * (f * parents + j)
-            moved = time & (LANES - 1)
-            first = jnp.take_along_axis(first, moved, axis=1, mode="promise_in_bounds")
-            second = jnp.take_along_axis(second, moved, axis=1, mode="promise_in_bounds")
-            inside = time < LANES
-            first = jnp.where(inside, first, jnp.where(time < 2 * LANES, second, 0.0))
-            second = jnp.where(inside, second, 0.0)
-            skewed[0, at, :] = first
-            skewed[1, at, :] = second
-        return carry
-
-    lax.fori_loop(0, parents // SKEW, skew, 0)
+    upper = sub >= 4
+    row = sub & 3
+
+    pace = f * 4 + row
+    begin = lane + jnp.where(upper, 64 * pace, 0)
+    rows = []
+    for u in range(64):
+        here, there = u * 8, (u + 64) * 8
+        first = jnp.where(upper, rows32[there - 4 : there + 4, :], rows32[here : here + 8, :])
+        second = jnp.where(upper, rows32[there : there + 8, :], rows32[here + 4 : here + 12, :])
+        time, begin = begin, begin + pace
+        moved = time & (LANES - 1)
+        inside = time < LANES
+        first = jnp.take_along_axis(first, moved, axis=1, mode="promise_in_bounds")
+        second = jnp.take_along_axis(second, moved, axis=1, mode="promise_in_bounds")
+        first = jnp.where(inside, first, jnp.where(time < 2 * LANES, second, 0.0))
+        rows.append((first, jnp.where(inside, second, 0.0)))
 
     def ahead(pair, s):
         return shifted(*pair, LANES - s, lane < LANES - s) if s else pair
 
-    def added(low, high):
-        return low[0] + high[0], low[1] + high[1]
-
-    def last_levels(block, carry):
-        for n in range(TAIL):
-            last_tile(block * TAIL + n)
-        return carry
-
-    def last_tile(jt):
-        tiles = []
-        for band in range(8):
-            at = pl.ds(jt * 64 + band, 8, stride=8)
-            tiles.append((skewed[0, at, :], skewed[1, at, :]))
-        l12 = [[added(tiles[2 * k], ahead(tiles[2 * k + 1], e)) for e in range(2)] for k in range(4)]
-        l13 = [
-            [added(l12[2 * k][e >> 1], ahead(l12[2 * k + 1][e >> 1], (e + 1) // 2)) for e in range(4)]
-            for k in range(2)
-        ]
-        for c in range(8):
-            pair = added(l13[0][c >> 1], ahead(l13[1][c >> 1], (c + 1) // 2))
-            at = pl.ds(jt * 64 + c, 8, stride=8)
-            for h in range(2):
-                trials[h, at, :] = pair[h]
-
-    lax.fori_loop(0, 8 // TAIL, last_levels, 0)
+    for k in range(6):
+        width = 1 << k
+        grown = []
+        for u in range(32 >> k):
+            for c in range(width):
+                low = rows[2 * u * width + c]
+                high = rows[2 * u * width + c + width]
+                for e in range(2):
+                    moved = ahead(high, c + e)
+                    grown.append((low[0] + moved[0], low[1] + moved[1]))
+        rows = grown
+        if k == 3:
+            for n, pair in enumerate(rows):
+                for h in range(2):
+                    level11[h, n * 8 : n * 8 + 8, :] = pair[h]
+            rows = [tuple(level11[h, n * 8 : n * 8 + 8, :] for h in range(2)) for n in range(64)]
+
+    for c in range(64):
+        halves = [rows[c][h] for h in range(2)]
+        turned = [pltpu.roll(v, 4, 0) for v in halves]
+        pair = [jnp.where(upper, v, t) for v, t in zip(halves, turned)]
+        even, odd = ahead(pair, c), ahead(pair, c + 1)
+        for h in range(2):
+            low = jnp.where(upper, turned[h], halves[h])
+            trials[h, c * 8 : c * 8 + 8, :] = low + jnp.where(upper, odd[h], even[h])
 
     count = trials.shape[1]
     samples = 2 * LANES
-    top = prefix.shape[1]
+    span = prefix.shape[0] // 8
     parts = []
     for h in range(2):
         d = trials[h]
@@ -191,25 +154,44 @@
     time = lax.broadcasted_iota(jnp.int32, size, 1) & (samples - 1)
     lower = jnp.where(time < step, 1.0, 0.0).astype(jnp.bfloat16)
     summed = lax.dot_general(lower, values, (((1,), (1,)), ((), ())), preferred_element_type=jnp.float32)
-    for lt in range(count // LANES):
-        prefix[lt, : samples + 8, :] = summed[: samples + 8, lt * LANES : (lt + 1) * LANES]
-        prefix[lt, samples : samples + 8, :] = jnp.where(
-            sub == 0, summed[samples : samples + 8, lt * LANES : (lt + 1) * LANES], -jnp.inf
-        )
-        prefix[lt, samples + 8 :, :] = jnp.full((top - samples - 8, LANES), -jnp.inf, jnp.float32)
+    least = jnp.full((8, LANES), -jnp.inf, jnp.float32)
+    for tile in range(count // LANES):
+        for t in range(0, samples + 64, 8):
+            part = least
+            if t <= samples:
+                part = summed[t : t + 8, tile * LANES : (tile + 1) * LANES]
+            if t == samples:
+                part = jnp.where(sub == 0, part, least)
+            if t < span:
+                prefix[pl.ds(t * 8 + tile, 8, stride=8), :] = part
+            if t >= LANES:
+                prefix[pl.ds((t - LANES) * 8 + 4 + tile, 8, stride=8), :] = part
     copy.wait()
-    for lt in range(count // LANES):
-        starts = [prefix[lt, t : t + 8, :] for t in range(0, samples, 8)]
-        best = None
-        for k in range(widths.shape[0]):
-            w = widths[k]
-            peak = None
+
+    def boxcars(block, peaks):
+        base = pl.multiple_of(block * 256, 256)
+        starts = [prefix[pl.ds(base + t * 8, 8), :] for t in range(32)]
+        out = []
+        for k in range(WIDTHS):
+            w = pl.multiple_of(base + widths[k] * 8, 8)
+            two = [peaks[k], None]
             for n, start in enumerate(starts):
-                box = prefix[lt, pl.ds(8 * n + w, 8), :] - start
-                peak = box if peak is None else jnp.maximum(peak, box)
-            peak = peak * lax.rsqrt(jnp.full((8, LANES), w * CHANS, jnp.int32).astype(jnp.float32))
-            best = peak if best is None else jnp.maximum(best, peak)
-        out_ref[:, lt * LANES : (lt + 1) * LANES] = jnp.max(best, axis=0, keepdims=True)
+                box = prefix[pl.ds(w + n * 8, 8), :] - start
+                two[n % 2] = box if two[n % 2] is None else jnp.maximum(two[n % 2], box)
+            out.append(jnp.maximum(*two))
+        return tuple(out)
+
+    peaks = lax.fori_loop(0, 4, boxcars, (least,) * WIDTHS)
+    best = least
+    for k in range(WIDTHS):
+        norm = lax.rsqrt(jnp.full((8, LANES), widths[k] * CHANS, jnp.int32).astype(jnp.float32))
+        best = jnp.maximum(best, peaks[k] * norm)
+    best = jnp.maximum(best, pltpu.roll(best, 4, 0))
+    for i in range(count // LANES):
+        place = (lane >> 1) * 8 + (lane & 1) * 4 + i
+        found = jnp.take_along_axis(best, place & (LANES - 1), axis=1, mode="promise_in_bounds")
+        found = jnp.where(sub == place // LANES, found, least)
+        out_ref[:, i * LANES : (i + 1) * LANES] = jnp.max(found, axis=0, keepdims=True)
 
 
 def in_hbm(array):
@@ -248,8 +230,7 @@
             pltpu.VMEM((devices * 8, LANES), jnp.float32),
             pltpu.VMEM((2, 512, LANES), jnp.float32),
             pltpu.VMEM((2, 512, LANES), jnp.float32),
-            pltpu.VMEM((2, 512, LANES), jnp.float32),
-            pltpu.VMEM((4, 2 * LANES + 72, LANES), jnp.float32),
+            pltpu.VMEM((8 * (LANES + 64), LANES), jnp.float32),
         ],
         compiler_params=pltpu.CompilerParams(vmem_limit_bytes=32 * 1024 * 1024),
         name="trial_levels",

time: 28 us -> 27.6 us (0.986)
  Pallas kernels: 5.68 us -> 5.31 us
    pallas_call x1, Pallas kernels: 3.31 us -> 2.94 us  [shards(): pl.pallas_call(trial_kernel, out_shape=jax.ShapeDtypeStruct((1, 4 * LANES...]
where the time goes in v2:
time: 27.6 us; the launch traced here: 27.5 us
  blocking collectives  22.1 us (80%)
  Pallas kernels  5.31 us (19%)
    all_to_all x1, blocking collectives, shards(): lax.all_to_all(rows.reshape(devices, 8, LANES), ('freq', 'beam'), 0, 0, t...  22.1 us
    pallas_call x1, Pallas kernels, shards(): pl.pallas_call(trial_kernel, out_shape=jax.ShapeDtypeStruct((1, 4 * LANES...  2.94 us
    pallas_call x1, Pallas kernels, shards(): pl.pallas_call(channel_kernel, out_shape=jax.ShapeDtypeStruct((devices *...  2.37 us

profile of v2, /device:TPU:1, one launch (start us, length us, event | category | flops | bytes accessed | tf_op | source)
XLA Modules:
  0.0 27.5 jit_solution(12292863056604229579)
XLA Ops:
  0.0 2.4 %channel_levels.1 = bf16[1024,128]{1,0:T(8,128)(2,1)S(1)} custom-call(bf16[16,128,256]{2,1,0:T(8,128)(2,1)} %x_hbm.1, s32[16,128]{1,0:T(8,128)} %bitcast.5), custom_call_target="tpu_custom_call" | custom-call | tf_op jit(solution)/shard_map/channel_levels/pallas_call | solution.py:204
  2.4 22.1 %all_to_all.5 = bf16[128,8,128]{2,1,0:T(8,128)(2,1)S(1)} all-to-all(bf16[128,8,128]{2,1,0:T(8,128)(2,1)S(1)} %bitcast.3), channel_id=1, replica_groups=mesh['beam'=16,'freq'=8] {'freq','beam'}, dimensions={0} | all-to-all | bytes 524288 | tf_op jit(solution)/shard_map/all_to_all | solution.py:221
  24.5 2.9 %trial_levels.1 = f32[1,512]{1,0:T(1,128)} custom-call(bf16[1024,128]{1,0:T(8,128)(2,1)S(1)} %bitcast.4, s32[9]{0:T(128)} %widths_hbm.1), custom_call_target="tpu_custom_call" | custom-call | tf_op jit(solution)/shard_map/trial_levels/pallas_call | solution.py:222

commit v3 on v2

--- a/solution.py
+++ b/solution.py
@@ -135,10 +135,13 @@
         halves = [rows[c][h] for h in range(2)]
         turned = [pltpu.roll(v, 4, 0) for v in halves]
         pair = [jnp.where(upper, v, t) for v, t in zip(halves, turned)]
-        even, odd = ahead(pair, c), ahead(pair, c + 1)
+        time = lane + (sub >> 2) + c
+        moved = time & (LANES - 1)
+        inside = time < LANES
+        first, second = (jnp.take_along_axis(v, moved, axis=1, mode="promise_in_bounds") for v in pair)
+        moved = jnp.where(inside, first, second), jnp.where(inside, second, 0.0)
         for h in range(2):
-            low = jnp.where(upper, turned[h], halves[h])
-            trials[h, c * 8 : c * 8 + 8, :] = low + jnp.where(upper, odd[h], even[h])
+            trials[h, c * 8 : c * 8 + 8, :] = jnp.where(upper, turned[h], halves[h]) + moved[h]
 
     count = trials.shape[1]
     samples = 2 * LANES

time: 27.6 us -> 27.4 us (level)
  no operation moved by 1% of the time
where the time goes in v3:
time: 27.4 us; the launch traced here: 27.3 us
  blocking collectives  22.1 us (81%)
  Pallas kernels  5.13 us (19%)
    all_to_all x1, blocking collectives, shards(): lax.all_to_all(rows.reshape(devices, 8, LANES), ('freq', 'beam'), 0, 0, t...  22.1 us
    pallas_call x1, Pallas kernels, shards(): pl.pallas_call(trial_kernel, out_shape=jax.ShapeDtypeStruct((1, 4 * LANES...  2.76 us
    pallas_call x1, Pallas kernels, shards(): pl.pallas_call(channel_kernel, out_shape=jax.ShapeDtypeStruct((devices *...  2.37 us

profile of v3, /device:TPU:1, one launch (start us, length us, event | category | flops | bytes accessed | tf_op | source)
XLA Modules:
  0.0 27.3 jit_solution(7409994848331101092)
XLA Ops:
  0.0 2.4 %channel_levels.1 = bf16[1024,128]{1,0:T(8,128)(2,1)S(1)} custom-call(bf16[16,128,256]{2,1,0:T(8,128)(2,1)} %x_hbm.1, s32[16,128]{1,0:T(8,128)} %bitcast.5), custom_call_target="tpu_custom_call" | custom-call | tf_op jit(solution)/shard_map/channel_levels/pallas_call | solution.py:207
  2.4 22.1 %all_to_all.5 = bf16[128,8,128]{2,1,0:T(8,128)(2,1)S(1)} all-to-all(bf16[128,8,128]{2,1,0:T(8,128)(2,1)S(1)} %bitcast.3), channel_id=1, replica_groups=mesh['beam'=16,'freq'=8] {'freq','beam'}, dimensions={0} | all-to-all | bytes 524288 | tf_op jit(solution)/shard_map/all_to_all | solution.py:224
  24.5 2.8 %trial_levels.1 = f32[1,512]{1,0:T(1,128)} custom-call(bf16[1024,128]{1,0:T(8,128)(2,1)S(1)} %bitcast.4, s32[9]{0:T(128)} %widths_hbm.1), custom_call_target="tpu_custom_call" | custom-call | tf_op jit(solution)/shard_map/trial_levels/pallas_call | solution.py:225

commit v4 on v3

--- a/solution.py
+++ b/solution.py
@@ -86,7 +86,7 @@
     out_ref[...] = rows32[...].astype(jnp.bfloat16)
 
 
-def trial_kernel(rows_ref, widths_hbm, out_ref, widths, sem, rows32, level11, trials, prefix):
+def trial_kernel(rows_ref, widths_hbm, out_ref, widths, sem, rows32, trials, prefix):
     copy = pltpu.make_async_copy(widths_hbm, widths, sem)
     copy.start()
     f = lax.axis_index("freq")
@@ -125,11 +125,6 @@
                     moved = ahead(high, c + e)
                     grown.append((low[0] + moved[0], low[1] + moved[1]))
         rows = grown
-        if k == 3:
-            for n, pair in enumerate(rows):
-                for h in range(2):
-                    level11[h, n * 8 : n * 8 + 8, :] = pair[h]
-            rows = [tuple(level11[h, n * 8 : n * 8 + 8, :] for h in range(2)) for n in range(64)]
 
     for c in range(64):
         halves = [rows[c][h] for h in range(2)]
@@ -172,7 +167,7 @@
     copy.wait()
 
     def boxcars(block, peaks):
-        base = pl.multiple_of(block * 256, 256)
+        base = block * 256
         starts = [prefix[pl.ds(base + t * 8, 8), :] for t in range(32)]
         out = []
         for k in range(WIDTHS):
@@ -184,7 +179,9 @@
             out.append(jnp.maximum(*two))
         return tuple(out)
 
-    peaks = lax.fori_loop(0, 4, boxcars, (least,) * WIDTHS)
+    peaks = (least,) * WIDTHS
+    for block in range(4):
+        peaks = boxcars(block, peaks)
     best = least
     for k in range(WIDTHS):
         norm = lax.rsqrt(jnp.full((8, LANES), widths[k] * CHANS, jnp.int32).astype(jnp.float32))
@@ -232,7 +229,6 @@
             pltpu.SemaphoreType.DMA,
             pltpu.VMEM((devices * 8, LANES), jnp.float32),
             pltpu.VMEM((2, 512, LANES), jnp.float32),
-            pltpu.VMEM((2, 512, LANES), jnp.float32),
             pltpu.VMEM((8 * (LANES + 64), LANES), jnp.float32),
         ],
         compiler_params=pltpu.CompilerParams(vmem_limit_bytes=32 * 1024 * 1024),

time: 27.4 us -> 27.4 us (level)
  no operation moved by 1% of the time
where the time goes in v4:
time: 27.4 us; the launch traced here: 27.3 us
  blocking collectives  22.1 us (81%)
  Pallas kernels  5.16 us (19%)
    all_to_all x1, blocking collectives, shards(): lax.all_to_all(rows.reshape(devices, 8, LANES), ('freq', 'beam'), 0, 0, t...  22.1 us
    pallas_call x1, Pallas kernels, shards(): pl.pallas_call(trial_kernel, out_shape=jax.ShapeDtypeStruct((1, 4 * LANES...  2.79 us
    pallas_call x1, Pallas kernels, shards(): pl.pallas_call(channel_kernel, out_shape=jax.ShapeDtypeStruct((devices *...  2.37 us

profile of v4, /device:TPU:1, one launch (start us, length us, event | category | flops | bytes accessed | tf_op | source)
XLA Modules:
  0.0 27.3 jit_solution(28682340644002952)
XLA Ops:
  0.0 2.4 %channel_levels.1 = bf16[1024,128]{1,0:T(8,128)(2,1)S(1)} custom-call(bf16[16,128,256]{2,1,0:T(8,128)(2,1)} %x_hbm.1, s32[16,128]{1,0:T(8,128)} %bitcast.5), custom_call_target="tpu_custom_call" | custom-call | tf_op jit(solution)/shard_map/channel_levels/pallas_call | solution.py:204
  2.4 22.1 %all_to_all.5 = bf16[128,8,128]{2,1,0:T(8,128)(2,1)S(1)} all-to-all(bf16[128,8,128]{2,1,0:T(8,128)(2,1)S(1)} %bitcast.3), channel_id=1, replica_groups=mesh['beam'=16,'freq'=8] {'freq','beam'}, dimensions={0} | all-to-all | bytes 524288 | tf_op jit(solution)/shard_map/all_to_all | solution.py:221
  24.5 2.8 %trial_levels.1 = f32[1,512]{1,0:T(1,128)} custom-call(bf16[1024,128]{1,0:T(8,128)(2,1)S(1)} %bitcast.4, s32[9]{0:T(128)} %widths_hbm.1), custom_call_target="tpu_custom_call" | custom-call | tf_op jit(solution)/shard_map/trial_levels/pallas_call | solution.py:222

commit v5 on v3

--- a/solution.py
+++ b/solution.py
@@ -151,12 +151,17 @@
         d = trials[h]
         high = d.astype(jnp.bfloat16)
         parts.append((high, (d - high.astype(jnp.float32)).astype(jnp.bfloat16)))
-    values = jnp.concatenate([parts[0][0], parts[1][0], parts[0][1], parts[1][1]], axis=1)
+    values = jnp.concatenate([*parts[0], *parts[1]], axis=1)
     size = (samples + 16, 4 * LANES)
     step = lax.broadcasted_iota(jnp.int32, size, 0)
-    time = lax.broadcasted_iota(jnp.int32, size, 1) & (samples - 1)
+    time = lax.broadcasted_iota(jnp.int32, size, 1)
+    time = (time & (LANES - 1)) + time // samples * LANES
     lower = jnp.where(time < step, 1.0, 0.0).astype(jnp.bfloat16)
-    summed = lax.dot_general(lower, values, (((1,), (1,)), ((), ())), preferred_element_type=jnp.float32)
+    both = (((1,), (1,)), ((), ()))
+    summed = jnp.concatenate([
+        lax.dot_general(lower[:LANES, :samples], values[:, :samples], both, preferred_element_type=jnp.float32),
+        lax.dot_general(lower[LANES:], values, both, preferred_element_type=jnp.float32),
+    ])
     least = jnp.full((8, LANES), -jnp.inf, jnp.float32)
     for tile in range(count // LANES):
         for t in range(0, samples + 64, 8):

time: 27.4 us -> 27.4 us (level)
  no operation moved by 1% of the time
where the time goes in v5:
time: 27.4 us; the launch traced here: 27.3 us
  blocking collectives  22.1 us (81%)
  Pallas kernels  5.13 us (19%)
    all_to_all x1, blocking collectives, shards(): lax.all_to_all(rows.reshape(devices, 8, LANES), ('freq', 'beam'), 0, 0, t...  22.1 us
    pallas_call x1, Pallas kernels, shards(): pl.pallas_call(trial_kernel, out_shape=jax.ShapeDtypeStruct((1, 4 * LANES...  2.76 us
    pallas_call x1, Pallas kernels, shards(): pl.pallas_call(channel_kernel, out_shape=jax.ShapeDtypeStruct((devices *...  2.37 us

profile of v5, /device:TPU:1, one launch (start us, length us, event | category | flops | bytes accessed | tf_op | source)
XLA Modules:
  0.0 27.3 jit_solution(9050256901262117828)
XLA Ops:
  0.0 2.4 %channel_levels.1 = bf16[1024,128]{1,0:T(8,128)(2,1)S(1)} custom-call(bf16[16,128,256]{2,1,0:T(8,128)(2,1)} %x_hbm.1, s32[16,128]{1,0:T(8,128)} %bitcast.5), custom_call_target="tpu_custom_call" | custom-call | tf_op jit(solution)/shard_map/channel_levels/pallas_call | solution.py:212
  2.4 22.1 %all_to_all.5 = bf16[128,8,128]{2,1,0:T(8,128)(2,1)S(1)} all-to-all(bf16[128,8,128]{2,1,0:T(8,128)(2,1)S(1)} %bitcast.3), channel_id=1, replica_groups=mesh['beam'=16,'freq'=8] {'freq','beam'}, dimensions={0} | all-to-all | bytes 524288 | tf_op jit(solution)/shard_map/all_to_all | solution.py:229
  24.5 2.8 %trial_levels.1 = f32[1,512]{1,0:T(1,128)} custom-call(bf16[1024,128]{1,0:T(8,128)(2,1)S(1)} %bitcast.4, s32[9]{0:T(128)} %widths_hbm.1), custom_call_target="tpu_custom_call" | custom-call | tf_op jit(solution)/shard_map/trial_levels/pallas_call | solution.py:230

commit v6 on v3

--- a/solution.py
+++ b/solution.py
@@ -116,14 +116,14 @@
 
     for k in range(6):
         width = 1 << k
-        grown = []
-        for u in range(32 >> k):
-            for c in range(width):
+        grown = [None] * 64
+        for c in range(width):
+            for u in range(32 >> k):
                 low = rows[2 * u * width + c]
                 high = rows[2 * u * width + c + width]
                 for e in range(2):
                     moved = ahead(high, c + e)
-                    grown.append((low[0] + moved[0], low[1] + moved[1]))
+                    grown[2 * u * width + 2 * c + e] = (low[0] + moved[0], low[1] + moved[1])
         rows = grown
         if k == 3:
             for n, pair in enumerate(rows):
@@ -172,7 +172,7 @@
     copy.wait()
 
     def boxcars(block, peaks):
-        base = pl.multiple_of(block * 256, 256)
+        base = block * 256
         starts = [prefix[pl.ds(base + t * 8, 8), :] for t in range(32)]
         out = []
         for k in range(WIDTHS):
@@ -184,7 +184,9 @@
             out.append(jnp.maximum(*two))
         return tuple(out)
 
-    peaks = lax.fori_loop(0, 4, boxcars, (least,) * WIDTHS)
+    peaks = (least,) * WIDTHS
+    for block in range(4):
+        peaks = boxcars(block, peaks)
     best = least
     for k in range(WIDTHS):
         norm = lax.rsqrt(jnp.full((8, LANES), widths[k] * CHANS, jnp.int32).astype(jnp.float32))

time: 27.4 us -> 27.4 us (level)
  no operation moved by 1% of the time
where the time goes in v6:
time: 27.4 us; the launch traced here: 27.3 us
  blocking collectives  22.1 us (81%)
  Pallas kernels  5.17 us (19%)
    all_to_all x1, blocking collectives, shards(): lax.all_to_all(rows.reshape(devices, 8, LANES), ('freq', 'beam'), 0, 0, t...  22.1 us
    pallas_call x1, Pallas kernels, shards(): pl.pallas_call(trial_kernel, out_shape=jax.ShapeDtypeStruct((1, 4 * LANES...  2.81 us
    pallas_call x1, Pallas kernels, shards(): pl.pallas_call(channel_kernel, out_shape=jax.ShapeDtypeStruct((devices *...  2.37 us

profile of v6, /device:TPU:1, one launch (start us, length us, event | category | flops | bytes accessed | tf_op | source)
XLA Modules:
  0.0 27.3 jit_solution(11214923375702761749)
XLA Ops:
  0.0 2.4 %channel_levels.1 = bf16[1024,128]{1,0:T(8,128)(2,1)S(1)} custom-call(bf16[16,128,256]{2,1,0:T(8,128)(2,1)} %x_hbm.1, s32[16,128]{1,0:T(8,128)} %bitcast.5), custom_call_target="tpu_custom_call" | custom-call | tf_op jit(solution)/shard_map/channel_levels/pallas_call | solution.py:209
  2.4 22.1 %all_to_all.5 = bf16[128,8,128]{2,1,0:T(8,128)(2,1)S(1)} all-to-all(bf16[128,8,128]{2,1,0:T(8,128)(2,1)S(1)} %bitcast.3), channel_id=1, replica_groups=mesh['beam'=16,'freq'=8] {'freq','beam'}, dimensions={0} | all-to-all | bytes 524288 | tf_op jit(solution)/shard_map/all_to_all | solution.py:226
  24.5 2.8 %trial_levels.1 = f32[1,512]{1,0:T(1,128)} custom-call(bf16[1024,128]{1,0:T(8,128)(2,1)S(1)} %bitcast.4, s32[9]{0:T(128)} %widths_hbm.1), custom_call_target="tpu_custom_call" | custom-call | tf_op jit(solution)/shard_map/trial_levels/pallas_call | solution.py:227
